TPU v7x, 768 devices: a whole 4x8x12 slice. The times are simulated.
768 devices in a mesh: fsdp: 96 (over z, y), grp: 8 (over x, core).
Axes of the slice: x: 4, y: 8, z: 12, core: 2. Of those that a mesh axis runs over, the one named last changes fastest.
Arguments:
- grad_shards: bfloat16 [75497472], P(('fsdp', 'grp')), may hold values from -0.3984375 to 0.3984375
- shard_length: int32 [768], replicated, may hold values from 32768 to 98304, as said below
- block_owner: int32 [192], replicated, may hold values from 0 to 767, as said below
- left_factor: bfloat16 [768, 512, 512], P(('fsdp', 'grp'))
- right_factor: bfloat16 [768, 512, 512], P(('fsdp', 'grp'))
- left_root: bfloat16 [768, 512, 512], P(('fsdp', 'grp'))
- right_root: bfloat16 [768, 512, 512], P(('fsdp', 'grp'))
Outputs:
- direction_shards: bfloat16 [75497472], P(('fsdp', 'grp'))
- new_left: bfloat16 [768, 512, 512], P(('fsdp', 'grp'))
- new_right: bfloat16 [768, 512, 512], P(('fsdp', 'grp'))
Inputs may be any that keep to these rules, and one draw needn't show every extreme that they name: shard_length[d] = 65536 + u_d - u_(d-1) with integers -16384 <= u_d <= 16384, u_(-1) = 0 and the last u = 0, so device d's shard ends at (d+1) * 65536 + u_d. `block_owner`: block k is owned by one of the devices 4 * k to 4 * k + 4 - 1 (devices numbered fsdp-major); a device owns at most one block.
All inputs are finite; a program needn't handle non-finite values.
Results may differ from a plain program's by a relative error of at most 0.0049.
Values may be sent and summed in bfloat16 or wider, within the bound.
A program may use at most 64 MiB of HBM per device.

v0:
```python
import functools

import jax
import jax.numpy as jnp
from jax import lax
from jax.experimental import pallas as pl
from jax.experimental.pallas import tpu as pltpu
from jax.sharding import PartitionSpec as P

B = 512
LANES = 128
PART = 128
EDGE = 32
WROWS = PART + 2 * EDGE
REST = PART - EDGE
FLAT = WROWS * B // LANES
SPLIT = B // LANES
PAD = 264
MESH = pl.DeviceIdType.MESH

NEAR_ROWS = 80
LAST = 64
OUTER_ROWS = 2 * NEAR_ROWS
THEIR_ROWS = 2 * PART + EDGE

LEFT, RIGHT, SIB, PREV, NEXT, ACROSS = 0, 1, 2, 4, 5, 6

(
    R_EDGES, R_MAIN, R_PART, R_SEAM, R_ACROSS, R_PREV, R_NEXT, R_FWD, R_LROOT, R_RROOT, R_SOON, R_LAST,
    R_BACK, R_HEAD, R_HELLO, R_THEIRS, R_PASSED, RECVS,
) = (0, 1, 2, 4, 6, 7, 8, 9, 13, 14, 15, 17, 19, 20, 22, 23, 25, 27)
SENDS = 30


def kernel(
    lens_hbm, owner_hbm, grad_hbm, lfac_hbm, rfac_hbm, lroot_hbm, rroot_hbm,
    dir_out, nl_out, nr_out,
    lens, owner, grad, shifted, edges, main, block, lroot, rroot, picked, ltheirs, rtheirs, lfac, rfac,
    pout, pown, pin, head_out, head_in, hello, zwin,
    in_sem, send_sem, recv_sem,
):
    f = lax.axis_index("fsdp")
    g = lax.axis_index("grp")
    nf = lax.axis_size("fsdp")
    ng = lax.axis_size("grp")
    me = f * ng + g
    part = g % 4
    core = g % 2
    chip = part // 2
    first = (3 - part) // 3
    final = part // 3
    outer = first + final
    inner = 1 - outer
    base = me - part
    has_prev = base > 0
    has_next = base + 4 < nf * ng
    is_outer = outer == 1
    is_inner = inner == 1
    gives = jnp.logical_and(base == 0, chip == 1)
    takes = jnp.logical_and(base == 0, chip == 0)
    sends_rows = jnp.logical_not(gives)
    gets_rows = jnp.logical_not(takes)
    gives_inner = jnp.logical_and(is_inner, gives)
    gives_outer = jnp.logical_and(is_outer, gives)
    takes_inner = jnp.logical_and(is_inner, takes)
    takes_outer = jnp.logical_and(is_outer, takes)
    gets_inner = jnp.logical_and(is_inner, gets_rows)
    gets_outer = jnp.logical_and(is_outer, gets_rows)
    beyond = jnp.logical_or(jnp.logical_and(chip == 0, has_prev), jnp.logical_and(chip == 1, has_next))
    outer_beyond = jnp.logical_and(is_outer, beyond)
    inner_prev = jnp.logical_and(is_inner, has_prev)
    inner_next = jnp.logical_and(is_inner, has_next)

    def device(index):
        index = index + ng
        return index // ng - 1, index % ng

    sib = (f, g + 1 - 2 * core)
    land = (f, g - part + 2 - chip)
    diag = (f, g - part + 3 - 3 * chip)
    sib_part = part + 1 - 2 * core
    other = 2 - 2 * chip

    def only(there, act):
        if there is None:
            act()
        else:
            pl.when(there)(act)

    def spot(start, size):
        return pl.ds(pl.multiple_of(start, 16), size)

    loads = []

    def load(src, dst):
        copy = pltpu.make_async_copy(src, dst, in_sem.at[len(loads)])
        copy.start()
        loads.append(copy)
        return copy

    sends = []

    def send(src, dst, to, arrival, there=None):
        copy = pltpu.make_async_remote_copy(
            src_ref=src,
            dst_ref=dst,
            send_sem=send_sem.at[len(sends)],
            recv_sem=recv_sem.at[arrival],
            device_id=to,
            device_id_type=MESH,
        )
        only(there, copy.start)
        sends.append((copy, there))
        return len(sends) - 1

    def sent(index):
        copy, there = sends[index]
        sends[index] = None
        only(there, copy.wait_send)

    def arrived(dst, arrival, here=None):
        copy = pltpu.make_async_remote_copy(
            src_ref=dst,
            dst_ref=dst,
            send_sem=send_sem.at[0],
            recv_sem=recv_sem.at[arrival],
            device_id=sib,
            device_id_type=MESH,
        )
        only(here, copy.wait_recv)

    load_grad = load(grad_hbm, grad)
    load_lens = load(lens_hbm, lens)

    barrier = pltpu.get_barrier_semaphore()
    for to, there in (
        (sib, is_inner),
        (land, is_inner),
        (diag, is_inner),
        (device(base - 1), inner_prev),
        (device(base + 4), inner_next),
        (device(base - 3 + 8 * chip), outer_beyond),
        (device(base - 2 + 8 * chip), outer_beyond),
    ):
        only(there, functools.partial(pl.semaphore_signal, barrier, 1, device_id=to, device_id_type=MESH))
    greetings = inner * (1 + has_prev.astype(jnp.int32) + has_next.astype(jnp.int32)) + outer * (
        2 + 2 * beyond.astype(jnp.int32)
    )

    def meet():
        pl.semaphore_wait(barrier, greetings)

    hello[0] = jnp.zeros(hello.shape[1:], hello.dtype)
    pl.when(is_outer)(meet)
    send(hello.at[0], hello.at[1], sib, R_HELLO, is_outer)
    send(lroot_hbm.at[0], lroot.at[1], sib, R_LROOT, is_outer)
    send(rroot_hbm.at[0], rroot.at[1], sib, R_RROOT, is_outer)

    load_owner = load(owner_hbm, owner)
    load_roots = [load(lroot_hbm.at[0], lroot.at[0]), load(rroot_hbm.at[0], rroot.at[0])]
    load_facs = [load(lfac_hbm.at[0], lfac), load(rfac_hbm.at[0], rfac)]

    load_lens.wait()
    counts = lens[...] - PART * B
    spots = lax.broadcasted_iota(jnp.int32, counts.shape, 0) * counts.shape[1] + lax.broadcasted_iota(
        jnp.int32, counts.shape, 1
    )

    def shift_of(index):
        return jnp.sum(jnp.where(spots < index, counts, 0))

    own_shift = shift_of(me)
    next_shift = shift_of(me + 1)
    start = jnp.clip(own_shift + EDGE * B, 0, 2 * EDGE * B)
    length = next_shift - own_shift + PART * B
    down = start // LANES
    along = start % LANES

    load_grad.wait()
    chunk = FLAT // 8
    for i in range(8):
        at = i * chunk
        shifted[pl.ds(PAD + at, chunk), :] = pltpu.roll(
            grad[pl.ds(at, chunk), :].astype(jnp.float32), along, 1
        )

    def window(row, size, *dsts):
        lane = lax.broadcasted_iota(jnp.int32, (size, LANES), 1)
        for j in range(SPLIT):
            here = shifted[pl.ds(PAD - down + row * SPLIT + j, size, stride=SPLIT), :]
            above = shifted[pl.ds(PAD - 1 - down + row * SPLIT + j, size, stride=SPLIT), :]
            value = jnp.where(lane < along, above, here).astype(jnp.bfloat16)
            for dst in dsts:
                dst[:, pl.ds(j * LANES, LANES)] = value

    window(0, EDGE, edges.at[LEFT])
    window(WROWS - EDGE, EDGE, edges.at[RIGHT])
    window(EDGE, PART, main, block.at[spot(part * PART, PART)])

    pl.when(is_inner)(meet)

    rest = core * EDGE
    send(main.at[spot(rest, REST)], block.at[spot(part * PART + rest, REST)], land, R_PART + core)
    send(edges.at[1 - chip], edges.at[ACROSS], land, R_ACROSS, is_inner)
    for i in (1, 2):
        send(edges.at[chip], edges.at[NEXT - chip], device(base - 4 + 8 * chip + i), R_NEXT - chip, outer_beyond)
    arrived(hello.at[1], R_HELLO, is_inner)
    send(edges.at[pl.ds(LEFT, 2)], edges.at[pl.ds(SIB, 2)], sib, R_EDGES)
    send(main, block.at[spot(part * PART, PART)], sib, R_MAIN)
    send(lroot_hbm.at[0], lroot.at[1], sib, R_LROOT, is_inner)
    send(rroot_hbm.at[0], rroot.at[1], sib, R_RROOT, is_inner)

    lines = lax.broadcasted_iota(jnp.int32, (EDGE, B), 0) * B + lax.broadcasted_iota(jnp.int32, (EDGE, B), 1)

    def merge(row, bound, slot, before):
        rows = spot(row, EDGE)
        here = block[rows, :].astype(jnp.float32)
        there = edges[slot].astype(jnp.float32)
        place = lines + row * B
        keep = place < bound if before else place >= bound
        block[rows, :] = jnp.where(keep, here, there).astype(jnp.bfloat16)

    pieces = (
        spot(other * PART, REST),
        spot(other * PART + PART + EDGE, REST),
        spot(other * PART + PART - EDGE, 2 * EDGE),
    )
    forwards = []

    def pass_on(there, prev_there, next_there):
        for i in range(2):
            arrived(block.at[pieces[i]], R_PART + i, there)
            forwards.append(send(block.at[pieces[i]], block.at[pieces[i]], sib, R_FWD + i, there))
        for i in range(2):
            rows = spot(other * PART + PART - EDGE + EDGE * i, EDGE)
            arrived(block.at[rows], R_SEAM + i, there)
        send(block.at[pieces[2]], block.at[pieces[2]], sib, R_FWD + 2, there)
        arrived(edges.at[ACROSS], R_ACROSS, there)
        arrived(edges.at[PREV], R_PREV, prev_there)
        arrived(edges.at[NEXT], R_NEXT, next_there)
        send(edges.at[pl.ds(PREV, 3)], edges.at[pl.ds(PREV, 3)], sib, R_FWD + 3, there)

    pass_on(takes_inner, jnp.logical_and(takes_inner, has_prev), jnp.logical_and(takes_inner, has_next))

    seam = 2 * chip * PART + PART
    seam_bound = seam * B + jnp.where(core == 0, next_shift, own_shift)
    arrived(edges.at[pl.ds(SIB, 2)], R_EDGES)
    arrived(block.at[spot(sib_part * PART, PART)], R_MAIN)
    merge(seam - EDGE, seam_bound, LEFT + SIB * (1 - core), True)
    merge(seam, seam_bound, RIGHT + SIB * core, False)
    seam_rows = spot(seam - EDGE + EDGE * core, EDGE)
    send(block.at[seam_rows], block.at[seam_rows], land, R_SEAM + core)

    load_owner.wait()
    owner_part = owner[me // 4] - base
    slot = jnp.where(owner_part == part, 0, 1)
    near = owner_part // 2 == chip
    owns = owner_part == part
    for copy in load_roots:
        copy.wait()
    arrived(lroot.at[1], R_LROOT, gives)
    arrived(rroot.at[1], R_RROOT, gives)

    @pl.when(gives_inner)
    def _():
        picked[...] = rroot[slot]

    @pl.when(gives_outer)
    def _():
        picked[pl.ds(0, THEIR_ROWS), :] = lroot[slot, pl.ds(0, THEIR_ROWS), :]

    send(picked, rtheirs, land, R_THEIRS, gives_inner)
    send(picked.at[pl.ds(0, THEIR_ROWS)], ltheirs, land, R_THEIRS + 1, gives_outer)

    bounds = [PART * B * j + shift_of(base + j) for j in (0, 2, 4)]

    pass_on(gets_inner, jnp.logical_and(gets_inner, has_prev), jnp.logical_and(gets_inner, has_next))
    for index in forwards:
        sent(index)
    for i in range(3):
        arrived(block.at[pieces[i]], R_FWD + i, is_outer)
    arrived(edges.at[pl.ds(PREV, 3)], R_FWD + 3, is_outer)

    merge(0, bounds[0], PREV, False)
    merge(2 * PART - EDGE, bounds[1], ACROSS - (ACROSS - SIB * core) * chip, True)
    merge(2 * PART, bounds[1], ACROSS - (ACROSS - RIGHT - SIB * (1 - core)) * (1 - chip), False)
    merge(4 * PART - EDGE, bounds[2], NEXT, True)

    arrived(lroot.at[1], R_LROOT, sends_rows)
    arrived(rroot.at[1], R_RROOT, sends_rows)

    def direction(*rows):
        lines = [lroot[slot, spot(row, size), :] for row, size in rows]
        left = lines[0] if len(lines) == 1 else jnp.concatenate(lines, axis=0)
        half = jnp.dot(left, block[...], preferred_element_type=jnp.float32).astype(jnp.bfloat16)
        return jnp.dot(half, rroot[slot], preferred_element_type=jnp.float32).astype(jnp.bfloat16)

    soon = (1 - chip) * (4 * PART - 2 * NEAR_ROWS + NEAR_ROWS * outer) + chip * NEAR_ROWS * inner
    last = (1 - chip) * (2 * PART - EDGE + LAST * outer) + chip * (2 * NEAR_ROWS + LAST * inner)

    @pl.when(is_inner)
    def _():
        ends = direction((0, EDGE), (4 * PART - EDGE, EDGE))
        head_out[0] = ends[:EDGE]
        head_out[1] = ends[EDGE:]

    send(head_out.at[0], head_in.at[chip], device(base - 1), R_HEAD + chip, inner_prev)
    send(head_out.at[1], head_in.at[chip], device(base + 4), R_HEAD + chip, inner_next)

    @pl.when(sends_rows)
    def _():
        pout[pl.ds(0, NEAR_ROWS), :] = direction((soon, NEAR_ROWS))

    send(pout.at[pl.ds(0, NEAR_ROWS)], pin.at[spot(soon, NEAR_ROWS)], land, R_SOON + core, sends_rows)

    @pl.when(sends_rows)
    def _():
        pout[pl.ds(NEAR_ROWS, LAST), :] = direction((last, LAST))

    send(pout.at[pl.ds(NEAR_ROWS, LAST)], pin.at[spot(last, LAST)], land, R_LAST + core, sends_rows)

    mine_at = part * PART - EDGE + EDGE * first - EDGE * final
    pown[...] = direction((mine_at, WROWS))

    for copy in load_facs:
        copy.wait()
    for dst, fac, dims in ((nl_out, lfac, (1, 1)), (nr_out, rfac, (0, 0))):
        for i in range(SPLIT):
            strip = pl.ds(i * LANES, LANES)
            one = block[strip, :] if dims[0] == 1 else block[:, strip]
            gram = lax.dot_general(
                one,
                block[...],
                (((dims[0],), (dims[1],)), ((), ())),
                preferred_element_type=jnp.float32,
            )
            fresh = 0.9 * fac[strip, :].astype(jnp.float32) + 0.1 * gram
            dst[0, strip, :] = jnp.where(owns, fresh, 0.0).astype(jnp.bfloat16)

    def sender_rows(whose):
        outer_there = (whose + chip) % 2
        near_at = chip * (4 * PART - 2 * NEAR_ROWS + NEAR_ROWS * outer_there) + (1 - chip) * NEAR_ROWS * (
            1 - outer_there
        )
        last_at = chip * (2 * PART - EDGE + LAST * outer_there) + (1 - chip) * (
            2 * NEAR_ROWS + LAST * (1 - outer_there)
        )
        return near_at, last_at

    for i in range(2):
        near_at, _ = sender_rows(i)
        arrived(pin.at[spot(near_at, NEAR_ROWS)], R_SOON + i, gets_inner)
    outer_rows = spot(chip * (4 * PART - OUTER_ROWS), OUTER_ROWS)
    send(pin.at[outer_rows], pin.at[outer_rows], sib, R_BACK, gets_inner)
    for i in range(2):
        _, last_at = sender_rows(i)
        arrived(pin.at[spot(last_at, LAST)], R_LAST + i, gets_inner)
    arrived(pin.at[outer_rows], R_BACK, gets_outer)
    for i, ref in ((1, ltheirs), (0, rtheirs)):
        arrived(ref, R_THEIRS + i, takes_inner)
        send(ref, ref, sib, R_PASSED + i, takes_inner)
        arrived(ref, R_PASSED + i, takes_outer)

    @pl.when(takes)
    def _():
        left = ltheirs[spot(part * (PART - EDGE), WROWS), :]
        half = jnp.dot(left, block[...], preferred_element_type=jnp.float32).astype(jnp.bfloat16)
        pin[spot(part * (PART - EDGE), WROWS), :] = jnp.dot(
            half, rtheirs[...], preferred_element_type=jnp.float32
        ).astype(jnp.bfloat16)


    def mine(at, row, size):
        return jnp.where(
            near,
            pown[spot(at, size), :].astype(jnp.float32),
            pin[spot(row, size), :].astype(jnp.float32),
        )

    def place(row, value):
        for j in range(SPLIT):
            zwin[pl.ds(row * SPLIT + j, value.shape[0], stride=SPLIT), :] = pltpu.roll(
                value[:, j * LANES : (j + 1) * LANES], (LANES - along) % LANES, 1
            )

    place(EDGE, mine(EDGE - EDGE * first + EDGE * final, part * PART, PART))
    for i in range(2):
        arrived(head_in.at[i], R_HEAD + i, outer_beyond)
    beside = jnp.clip(me // 4 - 1 + 2 * chip, 0, owner.shape[0] - 1)
    head = jnp.where(
        (owner[beside] - 4 * beside) // 2 == 0,
        head_in[0].astype(jnp.float32),
        head_in[1].astype(jnp.float32),
    )
    top = mine(EDGE * final, part * PART - EDGE + EDGE * first, EDGE)
    place(0, jnp.where(part == 0, head, top))
    bottom = mine(EDGE + PART - EDGE * first, part * PART + PART - EDGE * final, EDGE)
    place(EDGE + PART, jnp.where(part == 3, head, bottom))

    lane = lax.broadcasted_iota(jnp.int32, (chunk, LANES), 1)
    flat = lax.broadcasted_iota(jnp.int32, (chunk, LANES), 0) * LANES + lane
    for i in range(8):
        at = i * chunk
        here = zwin[pl.ds(down + at, chunk), :]
        below = zwin[pl.ds(down + at + 1, chunk), :]
        value = jnp.where(lane + along < LANES, here, below)
        value = jnp.where(flat + at * LANES < length, value, 0.0)
        dir_out[pl.ds(at, chunk), :] = value.astype(jnp.bfloat16)

    for pair in sends:
        if pair is not None:
            only(pair[1], pair[0].wait_send)


def hand_over(*refs):
    sem = refs[-1]
    copies = [pltpu.make_async_copy(refs[i], refs[3 + i], sem.at[i]) for i in range(3)]
    for copy in copies:
        copy.start()
    for copy in copies:
        copy.wait()


def local(grad_shards, shard_length, block_owner, left_factor, right_factor, left_root, right_root):
    count = shard_length.shape[0]
    wide = LANES if count % LANES == 0 else count
    bf16 = jnp.bfloat16
    square = jax.ShapeDtypeStruct((1, B, B), bf16)
    call = pl.pallas_call(
        kernel,
        out_shape=(
            pltpu.VMEM((FLAT, LANES), bf16), pltpu.VMEM((1, B, B), bf16), pltpu.VMEM((1, B, B), bf16)
        ),
        in_specs=[pl.BlockSpec(memory_space=pl.ANY)] * 7,
        out_specs=[pl.BlockSpec(memory_space=pltpu.VMEM)] * 3,
        scratch_shapes=[
            pltpu.VMEM((count // wide, wide), jnp.int32),
            pltpu.SMEM(block_owner.shape, jnp.int32),
            pltpu.VMEM((FLAT, LANES), bf16),
            pltpu.VMEM((PAD + FLAT, LANES), jnp.float32),
            pltpu.VMEM((7, EDGE, B), bf16),
            pltpu.VMEM((PART, B), bf16),
            pltpu.VMEM((B, B), bf16),
            pltpu.VMEM((2, B, B), bf16),
            pltpu.VMEM((2, B, B), bf16),
            pltpu.VMEM((B, B), bf16),
            pltpu.VMEM((THEIR_ROWS, B), bf16),
            pltpu.VMEM((B, B), bf16),
            pltpu.VMEM((B, B), bf16),
            pltpu.VMEM((B, B), bf16),
            pltpu.VMEM((NEAR_ROWS + LAST, B), bf16),
            pltpu.VMEM((WROWS, B), bf16),
            pltpu.VMEM((B, B), bf16),
            pltpu.VMEM((2, EDGE, B), bf16),
            pltpu.VMEM((2, EDGE, B), bf16),
            pltpu.VMEM((2, 16, LANES), bf16),
            pltpu.VMEM((FLAT + PAD, LANES), jnp.float32),
            pltpu.SemaphoreType.DMA((7,)),
            pltpu.SemaphoreType.DMA((SENDS,)),
            pltpu.SemaphoreType.DMA((RECVS,)),
        ],
        compiler_params=pltpu.CompilerParams(
            collective_id=0, has_side_effects=True, vmem_limit_bytes=48 * 1024 * 1024
        ),
        name="shampoo_step",
    )
    given = (
        shard_length.reshape(count // wide, wide),
        block_owner,
        grad_shards.reshape(FLAT, LANES),
        left_factor,
        right_factor,
        left_root,
        right_root,
    )
    results = call(*(pltpu.with_memory_space_constraint(x, pltpu.HBM) for x in given))
    direction, new_left, new_right = pl.pallas_call(
        hand_over,
        out_shape=(jax.ShapeDtypeStruct((FLAT, LANES), bf16), square, square),
        in_specs=[pl.BlockSpec(memory_space=pltpu.VMEM)] * 3,
        out_specs=[pl.BlockSpec(memory_space=pl.ANY)] * 3,
        scratch_shapes=[pltpu.SemaphoreType.DMA((3,))],
        compiler_params=pltpu.CompilerParams(vmem_limit_bytes=16 * 1024 * 1024),
        name="hand_over",
    )(*(pltpu.with_memory_space_constraint(x, pltpu.VMEM) for x in results))
    return direction.reshape(grad_shards.shape), new_left, new_right


def solution(mesh):
    flat = P(("fsdp", "grp"))
    square = P(("fsdp", "grp"), None, None)
    return jax.shard_map(
        local,
        mesh=mesh,
        in_specs=(flat, P(), P(), square, square, square, square),
        out_specs=(flat, square, square),
        check_vma=False,
    )
```

profile of v0, /device:TPU:1, one launch (start us, length us, event | category | flops | bytes accessed | tf_op | source)
XLA Modules:
  0.0 22.6 jit_solution(16531494781162482855)
XLA Ops:
  0.6 20.9 %shampoo_step.1 = (bf16[768,128]{1,0:T(8,128)(2,1)S(1)}, bf16[1,512,512]{2,1,0:T(8,128)(2,1)S(1)}, bf16[1,512,512]{2,1,0:T(8,128)(2,1)S(1)}) custom-call(s32[6,128]{1,0:T(8,128)} %bitcast.4, s32[192]{0:T(256)} %owner_hbm.1, bf16[768,128]{1,0:T(8,128)(2,1)} %bitcast.3, bf16[1,512,512]{2,1,0:T(8,128)(2,1)} %lfac_hbm.1, bf16[1,512,512]{2,1,0:T(8,128)(2,1)} %rfac_hbm.1, ...), custom_call_target="tpu_custom_call" | custom-call | tf_op jit(solution)/shard_map/shampoo_step/pallas_call | solution.py:476
  21.5 1.1 %hand_over.1 = (bf16[768,128]{1,0:T(8,128)(2,1)}, bf16[1,512,512]{2,1,0:T(8,128)(2,1)}, bf16[1,512,512]{2,1,0:T(8,128)(2,1)}) custom-call(bf16[768,128]{1,0:T(8,128)(2,1)S(1)} %get-tuple-element.9.refs_0_, bf16[1,512,512]{2,1,0:T(8,128)(2,1)S(1)} %get-tuple-element.10.refs_1_, bf16[1,512,512]{2,1,0:T(8,128)(2,1)S(1)} %get-tuple-element.11.refs_2_), custom_call_target="tpu_custom_call" | custom-call | tf_op jit(solution)/shard_map/hand_over/pallas_call | solution.py:477
where the time goes:
time: 22.7 us; the launch traced here: 22.6 us
  Pallas kernels  21.9 us (96%)
  between operations  0.64 us (3%)
    pallas_call x1, Pallas kernels, local(): call(*(pltpu.with_memory_space_constraint(x, pltpu.HBM) for x in given))  20.9 us
    pallas_call x1, Pallas kernels, local(): pl.pallas_call(hand_over, out_shape=(jax.ShapeDtypeStruct((FLAT, LANES),...  1.06 us

commit v1 on v0

--- a/solution.py
+++ b/solution.py
@@ -36,7 +36,7 @@
     lens_hbm, owner_hbm, grad_hbm, lfac_hbm, rfac_hbm, lroot_hbm, rroot_hbm,
     dir_out, nl_out, nr_out,
     lens, owner, grad, shifted, edges, main, block, lroot, rroot, picked, ltheirs, rtheirs, lfac, rfac,
-    pout, pown, pin, head_out, head_in, hello, zwin,
+    pout, pown, pin, head_out, head_in, hello, halfway, zwin,
     in_sem, send_sem, recv_sem,
 ):
     f = lax.axis_index("fsdp")
@@ -60,6 +60,8 @@
     takes = jnp.logical_and(base == 0, chip == 0)
     sends_rows = jnp.logical_not(gives)
     gets_rows = jnp.logical_not(takes)
+    greets_sib = jnp.logical_or(is_inner, gets_rows)
+    early_roots = jnp.logical_and(is_outer, base == 0)
     gives_inner = jnp.logical_and(is_inner, gives)
     gives_outer = jnp.logical_and(is_outer, gives)
     takes_inner = jnp.logical_and(is_inner, takes)
@@ -134,7 +136,7 @@
 
     barrier = pltpu.get_barrier_semaphore()
     for to, there in (
-        (sib, is_inner),
+        (sib, greets_sib),
         (land, is_inner),
         (diag, is_inner),
         (device(base - 1), inner_prev),
@@ -143,7 +145,7 @@
         (device(base - 2 + 8 * chip), outer_beyond),
     ):
         only(there, functools.partial(pl.semaphore_signal, barrier, 1, device_id=to, device_id_type=MESH))
-    greetings = inner * (1 + has_prev.astype(jnp.int32) + has_next.astype(jnp.int32)) + outer * (
+    greetings = inner * (1 + gets_rows.astype(jnp.int32) + has_prev.astype(jnp.int32) + has_next.astype(jnp.int32)) + outer * (
         2 + 2 * beyond.astype(jnp.int32)
     )
 
@@ -152,9 +154,9 @@
 
     hello[0] = jnp.zeros(hello.shape[1:], hello.dtype)
     pl.when(is_outer)(meet)
-    send(hello.at[0], hello.at[1], sib, R_HELLO, is_outer)
-    send(lroot_hbm.at[0], lroot.at[1], sib, R_LROOT, is_outer)
-    send(rroot_hbm.at[0], rroot.at[1], sib, R_RROOT, is_outer)
+    send(hello.at[0], hello.at[1], sib, R_HELLO, takes_outer)
+    send(lroot_hbm.at[0], lroot.at[1], sib, R_LROOT, early_roots)
+    send(rroot_hbm.at[0], rroot.at[1], sib, R_RROOT, early_roots)
 
     load_owner = load(owner_hbm, owner)
     load_roots = [load(lroot_hbm.at[0], lroot.at[0]), load(rroot_hbm.at[0], rroot.at[0])]
@@ -204,11 +206,11 @@
     send(edges.at[1 - chip], edges.at[ACROSS], land, R_ACROSS, is_inner)
     for i in (1, 2):
         send(edges.at[chip], edges.at[NEXT - chip], device(base - 4 + 8 * chip + i), R_NEXT - chip, outer_beyond)
-    arrived(hello.at[1], R_HELLO, is_inner)
+    arrived(hello.at[1], R_HELLO, takes_inner)
     send(edges.at[pl.ds(LEFT, 2)], edges.at[pl.ds(SIB, 2)], sib, R_EDGES)
     send(main, block.at[spot(part * PART, PART)], sib, R_MAIN)
-    send(lroot_hbm.at[0], lroot.at[1], sib, R_LROOT, is_inner)
-    send(rroot_hbm.at[0], rroot.at[1], sib, R_RROOT, is_inner)
+    send(lroot_hbm.at[0], lroot.at[1], sib, R_LROOT, jnp.logical_not(early_roots))
+    send(rroot_hbm.at[0], rroot.at[1], sib, R_RROOT, jnp.logical_not(early_roots))
 
     lines = lax.broadcasted_iota(jnp.int32, (EDGE, B), 0) * B + lax.broadcasted_iota(jnp.int32, (EDGE, B), 1)
 
@@ -356,19 +358,27 @@
         _, last_at = sender_rows(i)
         arrived(pin.at[spot(last_at, LAST)], R_LAST + i, gets_inner)
     arrived(pin.at[outer_rows], R_BACK, gets_outer)
-    for i, ref in ((1, ltheirs), (0, rtheirs)):
+    def passed(ref, i):
         arrived(ref, R_THEIRS + i, takes_inner)
         send(ref, ref, sib, R_PASSED + i, takes_inner)
         arrived(ref, R_PASSED + i, takes_outer)
 
+    their_rows = spot(part * (PART - EDGE), WROWS)
+    passed(ltheirs, 1)
+
     @pl.when(takes)
     def _():
-        left = ltheirs[spot(part * (PART - EDGE), WROWS), :]
-        half = jnp.dot(left, block[...], preferred_element_type=jnp.float32).astype(jnp.bfloat16)
-        pin[spot(part * (PART - EDGE), WROWS), :] = jnp.dot(
-            half, rtheirs[...], preferred_element_type=jnp.float32
+        halfway[...] = jnp.dot(
+            ltheirs[their_rows, :], block[...], preferred_element_type=jnp.float32
         ).astype(jnp.bfloat16)
 
+    passed(rtheirs, 0)
+
+    @pl.when(takes)
+    def _():
+        pin[their_rows, :] = jnp.dot(
+            halfway[...], rtheirs[...], preferred_element_type=jnp.float32
+        ).astype(jnp.bfloat16)
 
     def mine(at, row, size):
         return jnp.where(
@@ -437,7 +447,7 @@
             pltpu.VMEM((count // wide, wide), jnp.int32),
             pltpu.SMEM(block_owner.shape, jnp.int32),
             pltpu.VMEM((FLAT, LANES), bf16),
-            pltpu.VMEM((PAD + FLAT, LANES), jnp.float32),
+            pltpu.VMEM((PAD + FLAT + 8, LANES), jnp.float32),
             pltpu.VMEM((7, EDGE, B), bf16),
             pltpu.VMEM((PART, B), bf16),
             pltpu.VMEM((B, B), bf16),
@@ -454,6 +464,7 @@
             pltpu.VMEM((2, EDGE, B), bf16),
             pltpu.VMEM((2, EDGE, B), bf16),
             pltpu.VMEM((2, 16, LANES), bf16),
+            pltpu.VMEM((WROWS, B), bf16),
             pltpu.VMEM((FLAT + PAD, LANES), jnp.float32),
             pltpu.SemaphoreType.DMA((7,)),
             pltpu.SemaphoreType.DMA((SENDS,)),

time: 22.7 us -> 22.7 us (level)
  no operation moved by 1% of the time
where the time goes in v1:
time: 22.7 us; the launch traced here: 22.6 us
  Pallas kernels  22 us (97%)
  between operations  0.64 us (3%)
    pallas_call x1, Pallas kernels, local(): call(*(pltpu.with_memory_space_constraint(x, pltpu.HBM) for x in given))  20.9 us
    pallas_call x1, Pallas kernels, local(): pl.pallas_call(hand_over, out_shape=(jax.ShapeDtypeStruct((FLAT, LANES),...  1.06 us

profile of v1, /device:TPU:1, one launch (start us, length us, event | category | flops | bytes accessed | tf_op | source)
XLA Modules:
  0.0 22.6 jit_solution(18375138366624114302)
XLA Ops:
  0.6 20.9 %shampoo_step.1 = (bf16[768,128]{1,0:T(8,128)(2,1)S(1)}, bf16[1,512,512]{2,1,0:T(8,128)(2,1)S(1)}, bf16[1,512,512]{2,1,0:T(8,128)(2,1)S(1)}) custom-call(s32[6,128]{1,0:T(8,128)} %bitcast.4, s32[192]{0:T(256)} %owner_hbm.1, bf16[768,128]{1,0:T(8,128)(2,1)} %bitcast.3, bf16[1,512,512]{2,1,0:T(8,128)(2,1)} %lfac_hbm.1, bf16[1,512,512]{2,1,0:T(8,128)(2,1)} %rfac_hbm.1, ...), custom_call_target="tpu_custom_call" | custom-call | tf_op jit(solution)/shard_map/shampoo_step/pallas_call | solution.py:487
  21.5 1.1 %hand_over.1 = (bf16[768,128]{1,0:T(8,128)(2,1)}, bf16[1,512,512]{2,1,0:T(8,128)(2,1)}, bf16[1,512,512]{2,1,0:T(8,128)(2,1)}) custom-call(bf16[768,128]{1,0:T(8,128)(2,1)S(1)} %get-tuple-element.9.refs_0_, bf16[1,512,512]{2,1,0:T(8,128)(2,1)S(1)} %get-tuple-element.10.refs_1_, bf16[1,512,512]{2,1,0:T(8,128)(2,1)S(1)} %get-tuple-element.11.refs_2_), custom_call_target="tpu_custom_call" | custom-call | tf_op jit(solution)/shard_map/hand_over/pallas_call | solution.py:488

commit v2 on v1

--- a/solution.py
+++ b/solution.py
@@ -394,6 +394,10 @@
             )
 
     place(EDGE, mine(EDGE - EDGE * first + EDGE * final, part * PART, PART))
+    top = mine(EDGE * final, part * PART - EDGE + EDGE * first, EDGE)
+    place(0, top)
+    bottom = mine(EDGE + PART - EDGE * first, part * PART + PART - EDGE * final, EDGE)
+    place(EDGE + PART, bottom)
     for i in range(2):
         arrived(head_in.at[i], R_HEAD + i, outer_beyond)
     beside = jnp.clip(me // 4 - 1 + 2 * chip, 0, owner.shape[0] - 1)
@@ -402,10 +406,14 @@
         head_in[0].astype(jnp.float32),
         head_in[1].astype(jnp.float32),
     )
-    top = mine(EDGE * final, part * PART - EDGE + EDGE * first, EDGE)
-    place(0, jnp.where(part == 0, head, top))
-    bottom = mine(EDGE + PART - EDGE * first, part * PART + PART - EDGE * final, EDGE)
-    place(EDGE + PART, jnp.where(part == 3, head, bottom))
+
+    @pl.when(part == 0)
+    def _():
+        place(0, head)
+
+    @pl.when(part == 3)
+    def _():
+        place(EDGE + PART, head)
 
     lane = lax.broadcasted_iota(jnp.int32, (chunk, LANES), 1)
     flat = lax.broadcasted_iota(jnp.int32, (chunk, LANES), 0) * LANES + lane

time: 22.7 us -> 22.7 us (level)
  no operation moved by 1% of the time
where the time goes in v2:
time: 22.7 us; the launch traced here: 22.6 us
  Pallas kernels  22 us (97%)
  between operations  0.64 us (3%)
    pallas_call x1, Pallas kernels, local(): call(*(pltpu.with_memory_space_constraint(x, pltpu.HBM) for x in given))  20.9 us
    pallas_call x1, Pallas kernels, local(): pl.pallas_call(hand_over, out_shape=(jax.ShapeDtypeStruct((FLAT, LANES),...  1.06 us

profile of v2, /device:TPU:1, one launch (start us, length us, event | category | flops | bytes accessed | tf_op | source)
XLA Modules:
  0.0 22.6 jit_solution(1667257958691118739)
XLA Ops:
  0.6 20.9 %shampoo_step.1 = (bf16[768,128]{1,0:T(8,128)(2,1)S(1)}, bf16[1,512,512]{2,1,0:T(8,128)(2,1)S(1)}, bf16[1,512,512]{2,1,0:T(8,128)(2,1)S(1)}) custom-call(s32[6,128]{1,0:T(8,128)} %bitcast.4, s32[192]{0:T(256)} %owner_hbm.1, bf16[768,128]{1,0:T(8,128)(2,1)} %bitcast.3, bf16[1,512,512]{2,1,0:T(8,128)(2,1)} %lfac_hbm.1, bf16[1,512,512]{2,1,0:T(8,128)(2,1)} %rfac_hbm.1, ...), custom_call_target="tpu_custom_call" | custom-call | tf_op jit(solution)/shard_map/shampoo_step/pallas_call | solution.py:495
  21.5 1.1 %hand_over.1 = (bf16[768,128]{1,0:T(8,128)(2,1)}, bf16[1,512,512]{2,1,0:T(8,128)(2,1)}, bf16[1,512,512]{2,1,0:T(8,128)(2,1)}) custom-call(bf16[768,128]{1,0:T(8,128)(2,1)S(1)} %get-tuple-element.9.refs_0_, bf16[1,512,512]{2,1,0:T(8,128)(2,1)S(1)} %get-tuple-element.10.refs_1_, bf16[1,512,512]{2,1,0:T(8,128)(2,1)S(1)} %get-tuple-element.11.refs_2_), custom_call_target="tpu_custom_call" | custom-call | tf_op jit(solution)/shard_map/hand_over/pallas_call | solution.py:496
